TPU v7x, 32 devices: a whole 2x2x4 slice. The times are simulated.
32 devices in a mesh: row: 8 (over z, x), col: 4 (over y, core).
Axes of the slice: x: 2, y: 2, z: 4, core: 2. Of those that a mesh axis runs over, the one named last changes fastest.
Arguments:
- state: float32 [3, 64, 64, 512], P(None, None, 'row', 'col'), may hold values from -1.5 to 3, as said below
- gauge_cells: int32 [8, 4, 2, 32], P('row', 'col'), may hold values from 0 to 1023
- gauge_count: int32 [8, 4, 2], P('row', 'col'), may hold values from 0 to 32, as said below
- obs_value: float32 [8, 4, 2, 32], P('row', 'col'), may hold values from 0.5 to 3
- obs_noise: float32 [8, 4, 2, 32, 64], P('row', 'col'), may hold values from -1.5 to 1.5
- obs_var: float32 [8, 4, 2, 32], P('row', 'col'), may hold values from 0.02 to 0.5
Outputs:
- analysis: float32 [3, 64, 64, 512], P(None, None, 'row', 'col')
Inputs may be any that keep to these rules, and one draw needn't show every extreme that they name: `state`: field 0 is depth, from 0.5 to 3.0; fields 1 and 2 are momenta, from -1.5 to 1.5. `gauge_count`: at most 32 live slots; in every batch some tile has all 32 slots live.
All inputs are finite; a program needn't handle non-finite values.
Results may differ from a plain program's by a relative error of at most 0.0003.
Values sent between devices are 32-bit elements; how exact they have to be, the bound alone decides.
A program may use at most 64 MiB of HBM per device.

v0:
```python
import jax
import jax.numpy as jnp
from jax import lax
from jax.sharding import PartitionSpec as P

BATCHES = 2
LOC = 6


gravity = 9.81
spacing = 2.0
timestep_length = 0.08


def extended(x, sides, width):
    for axis, dim in sides:
        devices, length = (lax.axis_size(axis), x.shape[dim])
        up = [(i, (i + 1) % devices) for i in range(devices - 1)]
        down = [(j, i) for i, j in up]
        last = lax.slice_in_dim(x, length - width, length, axis=dim)
        first = lax.slice_in_dim(x, 0, width, axis=dim)
        before = lax.ppermute(last, axis, up)
        after = lax.ppermute(first, axis, down)
        x = jnp.concatenate([before, x, after], axis=dim)
    return x


def unit_vector(normal_axis, rank_count):
    entries = [0.0, 1.0, 0.0] if normal_axis == 1 else [0.0, 0.0, 1.0]
    return jnp.array(entries, jnp.float32).reshape((3,) + (1,) * (rank_count - 1))


def physical_flux(values, normal_axis):
    water_depth = values[0]
    normal_vel = values[normal_axis] / water_depth
    pressure = 0.5 * gravity * water_depth * water_depth
    return values * normal_vel[None] + pressure[None] * unit_vector(normal_axis, values.ndim)


def hll_flux(lower, upper, normal_axis):
    speed_l = jnp.sqrt(gravity * lower[0])
    speed_r = jnp.sqrt(gravity * upper[0])
    vel_l = lower[normal_axis] / lower[0]
    vel_r = upper[normal_axis] / upper[0]
    slow_wave = jnp.minimum(jnp.minimum(vel_l - speed_l, vel_r - speed_r), 0.0)
    fast_wave = jnp.maximum(jnp.maximum(vel_l + speed_l, vel_r + speed_r), 0.0)
    numer = fast_wave[None] * physical_flux(lower, normal_axis) - slow_wave[None] * physical_flux(
        upper, normal_axis
    )
    numer = numer + (slow_wave * fast_wave)[None] * (upper - lower)
    return numer / (fast_wave - slow_wave)[None]


def state_tendency(padded):
    flux_c = hll_flux(padded[..., 1:-1, :-1], padded[..., 1:-1, 1:], 1)
    flux_r = hll_flux(padded[..., :-1, 1:-1], padded[..., 1:, 1:-1], 2)
    return (
        -(flux_c[..., 1:] - flux_c[..., :-1] + flux_r[..., 1:, :] - flux_r[..., :-1, :]) / spacing
    )


def walls(padded, rim_width, at_top, at_bottom, at_left, at_right):
    rank_count = padded.ndim
    sign_rows = jnp.array([1.0, 1.0, -1.0], jnp.float32).reshape((3,) + (1,) * (rank_count - 1))
    sign_cols = jnp.array([1.0, -1.0, 1.0], jnp.float32).reshape((3,) + (1,) * (rank_count - 1))
    mirror_top = jnp.flip(padded[..., rim_width : 2 * rim_width, :], axis=-2) * sign_rows
    padded = padded.at[..., :rim_width, :].set(
        jnp.where(at_top, mirror_top, padded[..., :rim_width, :])
    )
    mirror_bottom = jnp.flip(padded[..., -2 * rim_width : -rim_width, :], axis=-2) * sign_rows
    padded = padded.at[..., -rim_width:, :].set(
        jnp.where(at_bottom, mirror_bottom, padded[..., -rim_width:, :])
    )
    mirror_left = jnp.flip(padded[..., rim_width : 2 * rim_width], axis=-1) * sign_cols
    padded = padded.at[..., :rim_width].set(
        jnp.where(at_left, mirror_left, padded[..., :rim_width])
    )
    mirror_right = jnp.flip(padded[..., -2 * rim_width : -rim_width], axis=-1) * sign_cols
    padded = padded.at[..., -rim_width:].set(
        jnp.where(at_right, mirror_right, padded[..., -rim_width:])
    )
    return padded


def pack(
    prior_observation,
    slot_cells,
    live_count,
    obs_value,
    obs_noise,
    obs_var,
    tile_row,
    tile_col,
    tile_row_count,
    tile_column_count,
):
    member_states = prior_observation.shape[-1]
    slots = prior_observation.shape[-2]
    obs_anom = prior_observation - jnp.mean(prior_observation, axis=-1, keepdims=True)
    spread = jnp.sum(obs_anom * obs_anom, axis=-1) / (member_states - 1)
    live_mask = (jnp.arange(slots, dtype=jnp.int32) < live_count[..., None]).astype(jnp.float32)
    obs_weight = (
        live_mask[..., None]
        * (obs_value[..., None] + obs_noise - prior_observation)
        / (spread + obs_var)[..., None]
    )
    gauge_grid_row = tile_row * tile_row_count + slot_cells // tile_column_count
    gauge_column = tile_col * tile_column_count + slot_cells % tile_column_count
    coords = jnp.stack([gauge_grid_row, gauge_column], axis=-1).astype(jnp.float32)
    return (obs_anom, obs_weight, coords)


def increments(fields, cell_rows, cell_cols, obs_anom, obs_weight, coords):
    member_states = fields.shape[1]
    centered = fields - jnp.mean(fields, axis=1, keepdims=True)
    covariance = jnp.einsum("fmp,gm->fpg", centered, obs_anom, precision=lax.Precision.HIGHEST) / (
        member_states - 1
    )
    distance_sq = (cell_rows[:, None] - coords[None, :, 0]) ** 2 + (
        cell_cols[:, None] - coords[None, :, 1]
    ) ** 2
    taper_weight = jnp.maximum(1.0 - distance_sq / (LOC * LOC), 0.0) ** 2
    return jnp.einsum(
        "fpg,gm->fmp", covariance * taper_weight[None], obs_weight, precision=lax.Precision.HIGHEST
    )


def body(state, gauge_cells, gauge_count, obs_value, obs_noise, obs_var):
    member_states = state.shape[1]
    tile_row_count = state.shape[2]
    tile_column_count = state.shape[3]
    slots = gauge_cells.shape[3]
    tile_row = lax.axis_index("row")
    tile_col = lax.axis_index("col")
    at_top = tile_row == 0
    at_bottom = tile_row == lax.axis_size("row") - 1
    at_left = tile_col == 0
    at_right = tile_col == lax.axis_size("col") - 1

    def halo_padded(field_values):
        ghosted = extended(field_values, (("row", 2), ("col", 3)), 1)
        return walls(ghosted, 1, at_top, at_bottom, at_left, at_right)

    opening_section = state + timestep_length * state_tendency(halo_padded(state))
    predict_flood = 0.5 * (
        state + opening_section + timestep_length * state_tendency(halo_padded(opening_section))
    )
    flattened_state = predict_flood.reshape(3, member_states, tile_row_count * tile_column_count)
    rows_here = (tile_row * tile_row_count + jnp.arange(tile_row_count, dtype=jnp.int32)).astype(
        jnp.float32
    )
    cols_here = (
        tile_col * tile_column_count + jnp.arange(tile_column_count, dtype=jnp.int32)
    ).astype(jnp.float32)
    cell_rows = jnp.broadcast_to(rows_here[:, None], (tile_row_count, tile_column_count)).reshape(
        -1
    )
    cell_cols = jnp.broadcast_to(cols_here[None, :], (tile_row_count, tile_column_count)).reshape(
        -1
    )
    for batch in range(BATCHES):
        gauge_slot_cells = gauge_cells[0, 0, batch]
        point_rows = (tile_row * tile_row_count + gauge_slot_cells // tile_column_count).astype(
            jnp.float32
        )
        point_cols = (tile_col * tile_column_count + gauge_slot_cells % tile_column_count).astype(
            jnp.float32
        )
        slot_cells, point_rows, point_cols = (gauge_slot_cells, point_rows, point_cols)
        depth_at = jnp.take(flattened_state[0], slot_cells, axis=1)
        packets_slot_cells = gauge_cells[0, 0, batch]
        obs_anom, obs_weight, coords = pack(
            depth_at.T,
            packets_slot_cells,
            gauge_count[0, 0, batch],
            obs_value[0, 0, batch],
            obs_noise[0, 0, batch],
            obs_var[0, 0, batch],
            tile_row,
            tile_col,
            tile_row_count,
            tile_column_count,
        )
        near_anom = extended(obs_anom[None, None], (("row", 0), ("col", 1)), 1)
        near_weight = extended(obs_weight[None, None], (("row", 0), ("col", 1)), 1)
        near_coords = extended(coords[None, None], (("row", 0), ("col", 1)), 1)
        flattened_state = flattened_state + increments(
            flattened_state,
            cell_rows,
            cell_cols,
            near_anom.reshape(9 * slots, member_states),
            near_weight.reshape(9 * slots, member_states),
            near_coords.reshape(9 * slots, 2),
        )
    return flattened_state.reshape(3, member_states, tile_row_count, tile_column_count)


def solution(mesh):
    placed = (
        P(None, None, "row", "col"),
        P("row", "col", None, None),
        P("row", "col", None),
        P("row", "col", None, None),
        P("row", "col", None, None, None),
        P("row", "col", None, None),
    )
    return jax.shard_map(
        body, mesh=mesh, in_specs=placed, out_specs=P(None, None, "row", "col"), check_vma=False
    )
```

profile of v0, /device:TPU:17, one launch (start us, length us, event | category | flops | bytes accessed | tf_op | source)
XLA Modules:
  0.0 195.0 jit_solution(3233749332202725047)
XLA Ops:
  0.8 3.0 %collective-permute-start.29 = (f32[1,1,32,2]{2,3,1,0:T(2,128)S(1)}, f32[1,1,32,2]{2,3,1,0:T(2,128)S(1)}, u32[]{:S(2)}, u32[]{:S(2)}) collective-permute-start(f32[1,1,32,2]{2,3,1,0:T(2,128)S(1)} %add_convert_fusion.1), channel_id=1, source_target_pairs={{4,0},{8,4},{12,8},{16,12},{20,16},{24,20},{28,24},{5,1},{9,5},{13... | collective-permute-start | bytes 776 | tf_op jit(solution)/shard_map/ppermute | solution.py:23
  6.1 3.9 %collective-permute-start.17 = (f32[1,1,32,2]{2,3,1,0:T(2,128)S(1)}, f32[1,1,32,2]{2,3,1,0:T(2,128)S(1)}, u32[]{:S(2)}, u32[]{:S(2)}) collective-permute-start(f32[1,1,32,2]{2,3,1,0:T(2,128)S(1)} %add_convert_fusion), channel_id=1, source_target_pairs={{4,0},{8,4},{12,8},{16,12},{20,16},{24,20},{28,24},{5,1},{9,5},{13... | collective-permute-start | bytes 776 | tf_op jit(solution)/shard_map/ppermute | solution.py:23
  13.6 4.1 %collective-permute-start.1 = (f32[3,64,1,128]{3,1,2,0:T(8,128)S(1)}, f32[3,64,1,128]{3,1,2,0:T(8,128)S(1)}, u32[]{:S(2)}, u32[]{:S(2)}) collective-permute-start(f32[3,64,1,128]{3,1,2,0:T(8,128)S(1)} %bitcast.211), channel_id=1, source_target_pairs={{4,0},{8,4},{12,8},{16,12},{20,16},{24,20},{28,24},{5,1},{9,5},{13... | collective-permute-start | bytes 294920 | tf_op jit(solution)/shard_map/ppermute | solution.py:23
  23.8 4.0 %collective-permute-start.31 = (f32[3,1,32,2]{2,3,1,0:T(2,128)S(1)}, f32[3,1,32,2]{2,3,1,0:T(2,128)S(1)}, u32[]{:S(2)}, u32[]{:S(2)}) collective-permute-start(f32[3,1,32,2]{2,3,1,0:T(2,128)S(1)} %pad_maximum_fusion.19), channel_id=1, source_target_pairs={{1,0},{2,1},{3,2},{5,4},{6,5},{7,6},{9,8},{10,9},{11,10},{13,12},{... | collective-permute-start | bytes 2312 | tf_op jit(solution)/shard_map/ppermute | solution.py:23
  27.8 3.0 %collective-permute-start.30 = (f32[3,1,32,2]{2,3,1,0:T(2,128)S(1)}, f32[3,1,32,2]{2,3,1,0:T(2,128)S(1)}, u32[]{:S(2)}, u32[]{:S(2)}) collective-permute-start(f32[3,1,32,2]{2,3,1,0:T(2,128)S(1)} %pad_maximum_fusion.19), channel_id=1, source_target_pairs={{0,1},{1,2},{2,3},{4,5},{5,6},{6,7},{8,9},{9,10},{10,11},{12,13},{... | collective-permute-start | bytes 2312 | tf_op jit(solution)/shard_map/ppermute | solution.py:22
  32.8 3.6 %collective-permute-start.18 = (f32[3,1,32,2]{2,3,1,0:T(2,128)S(1)}, f32[3,1,32,2]{2,3,1,0:T(2,128)S(1)}, u32[]{:S(2)}, u32[]{:S(2)}) collective-permute-start(f32[3,1,32,2]{2,3,1,0:T(2,128)S(1)} %pad_maximum_fusion.18), channel_id=1, source_target_pairs={{0,1},{1,2},{2,3},{4,5},{5,6},{6,7},{8,9},{9,10},{10,11},{12,13},{... | collective-permute-start | bytes 2312 | tf_op jit(solution)/shard_map/ppermute | solution.py:22
  38.7 3.6 %collective-permute-start.2 = (f32[3,64,10,1]{1,2,3,0:T(8,128)S(1)}, f32[3,64,10,1]{1,2,3,0:T(8,128)S(1)}, u32[]{:S(2)}, u32[]{:S(2)}) collective-permute-start(f32[3,64,10,1]{1,2,3,0:T(8,128)S(1)} %get-tuple-element.148), channel_id=1, source_target_pairs={{0,1},{1,2},{2,3},{4,5},{5,6},{6,7},{8,9},{9,10},{10,11},{12,13},{... | collective-permute-start | bytes 23048 | tf_op jit(solution)/shard_map/ppermute | solution.py:22
  45.7 11.0 %scatter.26 = f32[3,64,10,130]{1,2,3,0:T(8,128)S(1)} dynamic-update-slice(f32[3,64,10,130]{1,2,3,0:T(8,128)S(1)} %pad_maximum_fusion, f32[3,64,1,130]{1,2,3,0:T(1,128)S(1)} %broadcast_select_fusion.3, s32[]{:T(128)} %constant.280.clone.1, s32[]{:T(128)} %constant.280.clone.1, s32[]{:T(128)} %constant.280.clone.1, s32[]{:T(128)} %constant.280.clone.1) | dynamic-update-slice | bytes 199684 | tf_op jit(solution)/shard_map/scatter | solution.py:67
  57.0 11.0 %scatter.29 = f32[3,64,10,130]{1,2,3,0:T(8,128)S(1)} dynamic-update-slice(f32[3,64,10,130]{1,2,3,0:T(8,128)S(1)} %scatter.26, f32[3,64,1,130]{1,2,3,0:T(1,128)S(1)} %broadcast_select_fusion.1, s32[]{:T(128)} %constant.280.clone.1, s32[]{:T(128)} %constant.280.clone.1, s32[]{:T(128)} %constant.282.clone.1, s32[]{:T(128)} %constant.280.clone.1) | dynamic-update-slice | bytes 199684 | tf_op jit(solution)/shard_map/scatter | solution.py:71
  74.5 4.4 %collective-permute-start.5 = (f32[3,64,1,128]{3,1,2,0:T(8,128)S(1)}, f32[3,64,1,128]{3,1,2,0:T(8,128)S(1)}, u32[]{:S(2)}, u32[]{:S(2)}) collective-permute-start(f32[3,64,1,128]{3,1,2,0:T(8,128)S(1)} %copy.124), channel_id=1, source_target_pairs={{4,0},{8,4},{12,8},{16,12},{20,16},{24,20},{28,24},{5,1},{9,5},{13... | collective-permute-start | bytes 294920 | tf_op jit(solution)/shard_map/ppermute | solution.py:23
  81.2 4.5 %collective-permute-done.4 = f32[3,64,1,128]{3,1,2,0:T(8,128)S(1)} collective-permute-done((f32[3,64,1,128]{3,1,2,0:T(8,128)S(1)}, f32[3,64,1,128]{3,1,2,0:T(8,128)S(1)}, u32[]{:S(2)}, u32[]{:S(2)}) %collective-permute-start.4) | collective-permute-done | bytes 98336 | tf_op jit(solution)/shard_map/ppermute | solution.py:22
  88.1 5.2 %collective-permute-start.6 = (f32[3,64,10,1]{1,2,3,0:T(8,128)S(1)}, f32[3,64,10,1]{1,2,3,0:T(8,128)S(1)}, u32[]{:S(2)}, u32[]{:S(2)}) collective-permute-start(f32[3,64,10,1]{1,2,3,0:T(8,128)S(1)} %get-tuple-element.146), channel_id=1, source_target_pairs={{0,1},{1,2},{2,3},{4,5},{5,6},{6,7},{8,9},{9,10},{10,11},{12,13},{... | collective-permute-start | bytes 23048 | tf_op jit(solution)/shard_map/ppermute | solution.py:22
  97.5 11.0 %scatter.34 = f32[3,64,10,130]{1,2,3,0:T(8,128)S(1)} dynamic-update-slice(f32[3,64,10,130]{1,2,3,0:T(8,128)S(1)} %pad_maximum_fusion.1, f32[3,64,1,130]{1,2,3,0:T(1,128)S(1)} %broadcast_select_fusion.2, s32[]{:T(128)} %constant.280.clone.1, s32[]{:T(128)} %constant.280.clone.1, s32[]{:T(128)} %constant.280.clone.1, s32[]{:T(128)} %constant.280.clone.1) | dynamic-update-slice | bytes 199684 | tf_op jit(solution)/shard_map/scatter | solution.py:67
  108.8 11.0 %scatter.35 = f32[3,64,10,130]{1,2,3,0:T(8,128)S(1)} dynamic-update-slice(f32[3,64,10,130]{1,2,3,0:T(8,128)S(1)} %scatter.34, f32[3,64,1,130]{1,2,3,0:T(1,128)S(1)} %broadcast_select_fusion, s32[]{:T(128)} %constant.280.clone.1, s32[]{:T(128)} %constant.280.clone.1, s32[]{:T(128)} %constant.282.clone.1, s32[]{:T(128)} %constant.280.clone.1) | dynamic-update-slice | bytes 199684 | tf_op jit(solution)/shard_map/scatter | solution.py:71
  129.3 3.4 %collective-permute-start.8 = (f32[1,1,32,64]{3,2,1,0:T(8,128)S(1)}, f32[1,1,32,64]{3,2,1,0:T(8,128)S(1)}, u32[]{:S(2)}, u32[]{:S(2)}) collective-permute-start(f32[1,1,32,64]{3,2,1,0:T(8,128)S(1)} %fusion.47), channel_id=1, source_target_pairs={{0,4},{4,8},{8,12},{12,16},{16,20},{20,24},{24,28},{1,5},{5,9},{9,... | collective-permute-start | bytes 24584 | tf_op jit(solution)/shard_map/ppermute | solution.py:22
  143.8 3.8 %collective-permute-start.14 = (f32[3,1,32,64]{3,2,1,0:T(8,128)S(1)}, f32[3,1,32,64]{3,2,1,0:T(8,128)S(1)}, u32[]{:S(2)}, u32[]{:S(2)}) collective-permute-start(f32[3,1,32,64]{3,2,1,0:T(8,128)S(1)} %pad_maximum_fusion.7), channel_id=1, source_target_pairs={{0,1},{1,2},{2,3},{4,5},{5,6},{6,7},{8,9},{9,10},{10,11},{12,13},{... | collective-permute-start | bytes 73736 | tf_op jit(solution)/shard_map/ppermute | solution.py:22
  149.6 3.9 %collective-permute-start.10 = (f32[3,1,32,64]{3,2,1,0:T(8,128)S(1)}, f32[3,1,32,64]{3,2,1,0:T(8,128)S(1)}, u32[]{:S(2)}, u32[]{:S(2)}) collective-permute-start(f32[3,1,32,64]{3,2,1,0:T(8,128)S(1)} %pad_maximum_fusion.6), channel_id=1, source_target_pairs={{0,1},{1,2},{2,3},{4,5},{5,6},{6,7},{8,9},{9,10},{10,11},{12,13},{... | collective-permute-start | bytes 73736 | tf_op jit(solution)/shard_map/ppermute | solution.py:22
  153.5 3.3 %fusion.66 = f32[3,1024,288]{1,2,0:T(8,128)S(1)} fusion(f32[3,64,1024]{2,1,0:T(8,128)S(1)} %sub.270, f32[288,64,1]{1,0,2:T(8,128)S(1)} %bitcast.208), kind=kOutput, calls=%fused_computation.197 | convolution fusion | flops 679477248 | bytes 4399104 | tf_op jit(solution)/shard_map/fmp,gm->fpg/dot_general | solution.py:116
  161.0 3.5 %collective-permute-start.21 = (f32[1,1,32,64]{3,2,1,0:T(8,128)S(1)}, f32[1,1,32,64]{3,2,1,0:T(8,128)S(1)}, u32[]{:S(2)}, u32[]{:S(2)}) collective-permute-start(f32[1,1,32,64]{3,2,1,0:T(8,128)S(1)} %fusion.43), channel_id=1, source_target_pairs={{4,0},{8,4},{12,8},{16,12},{20,16},{24,20},{28,24},{5,1},{9,5},{13... | collective-permute-start | bytes 24584 | tf_op jit(solution)/shard_map/ppermute | solution.py:23
  166.6 4.2 %collective-permute-start.25 = (f32[1,1,32,64]{3,2,1,0:T(8,128)S(1)}, f32[1,1,32,64]{3,2,1,0:T(8,128)S(1)}, u32[]{:S(2)}, u32[]{:S(2)}) collective-permute-start(f32[1,1,32,64]{3,2,1,0:T(8,128)S(1)} %get-tuple-element.154), channel_id=1, source_target_pairs={{4,0},{8,4},{12,8},{16,12},{20,16},{24,20},{28,24},{5,1},{9,5},{13... | collective-permute-start | bytes 24584 | tf_op jit(solution)/shard_map/ppermute | solution.py:23
  172.8 3.7 %collective-permute-done.24 = f32[1,1,32,64]{3,2,1,0:T(8,128)S(1)} collective-permute-done((f32[1,1,32,64]{3,2,1,0:T(8,128)S(1)}, f32[1,1,32,64]{3,2,1,0:T(8,128)S(1)}, u32[]{:S(2)}, u32[]{:S(2)}) %collective-permute-start.24) | collective-permute-done | bytes 8224 | tf_op jit(solution)/shard_map/ppermute | solution.py:22
  178.9 3.2 %collective-permute-start.26 = (f32[3,1,32,64]{3,2,1,0:T(8,128)S(1)}, f32[3,1,32,64]{3,2,1,0:T(8,128)S(1)}, u32[]{:S(2)}, u32[]{:S(2)}) collective-permute-start(f32[3,1,32,64]{3,2,1,0:T(8,128)S(1)} %pad_maximum_fusion.9), channel_id=1, source_target_pairs={{0,1},{1,2},{2,3},{4,5},{5,6},{6,7},{8,9},{9,10},{10,11},{12,13},{... | collective-permute-start | bytes 73736 | tf_op jit(solution)/shard_map/ppermute | solution.py:22
  184.1 3.6 %collective-permute-start.22 = (f32[3,1,32,64]{3,2,1,0:T(8,128)S(1)}, f32[3,1,32,64]{3,2,1,0:T(8,128)S(1)}, u32[]{:S(2)}, u32[]{:S(2)}) collective-permute-start(f32[3,1,32,64]{3,2,1,0:T(8,128)S(1)} %pad_maximum_fusion.8), channel_id=1, source_target_pairs={{0,1},{1,2},{2,3},{4,5},{5,6},{6,7},{8,9},{9,10},{10,11},{12,13},{... | collective-permute-start | bytes 73736 | tf_op jit(solution)/shard_map/ppermute | solution.py:22
  187.8 3.3 %fusion.29 = f32[3,1024,288]{1,2,0:T(8,128)S(1)} fusion(f32[288,64,1]{1,0,2:T(8,128)S(1)} %bitcast.209, f32[3,64,1024]{2,1,0:T(8,128)S(1)} %get-tuple-element.171, f32[3,1024]{1,0:T(4,128)S(1)} %broadcast_multiply_fusion.1), kind=kOutput, calls=%fused_computation.61 | convolution fusion | flops 679673856 | bytes 4411392 | tf_op jit(solution)/shard_map/fmp,gm->fpg/dot_general | solution.py:116
  (180 shorter events, 74.4 us)
Async XLA Ops:
  0.8 20.9 %collective-permute-start.29 = (f32[1,1,32,2]{2,3,1,0:T(2,128)S(1)}, f32[1,1,32,2]{2,3,1,0:T(2,128)S(1)}, u32[]{:S(2)}, u32[]{:S(2)}) collective-permute-start(f32[1,1,32,2]{2,3,1,0:T(2,128)S(1)} %add_convert_fusion.1), channel_id=1, source_target_pairs={{4,0},{8,4},{12,8},{16,12},{20,16},{24,20},{28,24},{5,1},{9,5},{13... | collective-permute-start | bytes 776 | tf_op jit(solution)/shard_map/ppermute | solution.py:23
  3.8 19.9 %collective-permute-start.28 = (f32[1,1,32,2]{2,3,1,0:T(2,128)S(1)}, f32[1,1,32,2]{2,3,1,0:T(2,128)S(1)}, u32[]{:S(2)}, u32[]{:S(2)}) collective-permute-start(f32[1,1,32,2]{2,3,1,0:T(2,128)S(1)} %add_convert_fusion.1), channel_id=1, source_target_pairs={{0,4},{4,8},{8,12},{12,16},{16,20},{20,24},{24,28},{1,5},{5,9},{9,... | collective-permute-start | bytes 776 | tf_op jit(solution)/shard_map/ppermute | solution.py:22
  6.1 21.6 %collective-permute-start.17 = (f32[1,1,32,2]{2,3,1,0:T(2,128)S(1)}, f32[1,1,32,2]{2,3,1,0:T(2,128)S(1)}, u32[]{:S(2)}, u32[]{:S(2)}) collective-permute-start(f32[1,1,32,2]{2,3,1,0:T(2,128)S(1)} %add_convert_fusion), channel_id=1, source_target_pairs={{4,0},{8,4},{12,8},{16,12},{20,16},{24,20},{28,24},{5,1},{9,5},{13... | collective-permute-start | bytes 776 | tf_op jit(solution)/shard_map/ppermute | solution.py:23
  10.0 20.8 %collective-permute-start.16 = (f32[1,1,32,2]{2,3,1,0:T(2,128)S(1)}, f32[1,1,32,2]{2,3,1,0:T(2,128)S(1)}, u32[]{:S(2)}, u32[]{:S(2)}) collective-permute-start(f32[1,1,32,2]{2,3,1,0:T(2,128)S(1)} %add_convert_fusion), channel_id=1, source_target_pairs={{0,4},{4,8},{8,12},{12,16},{16,20},{20,24},{24,28},{1,5},{5,9},{9,... | collective-permute-start | bytes 776 | tf_op jit(solution)/shard_map/ppermute | solution.py:22
  13.6 22.8 %collective-permute-start.1 = (f32[3,64,1,128]{3,1,2,0:T(8,128)S(1)}, f32[3,64,1,128]{3,1,2,0:T(8,128)S(1)}, u32[]{:S(2)}, u32[]{:S(2)}) collective-permute-start(f32[3,64,1,128]{3,1,2,0:T(8,128)S(1)} %bitcast.211), channel_id=1, source_target_pairs={{4,0},{8,4},{12,8},{16,12},{20,16},{24,20},{28,24},{5,1},{9,5},{13... | collective-permute-start | bytes 294920 | tf_op jit(solution)/shard_map/ppermute | solution.py:23
  21.7 14.9 %collective-permute-start = (f32[3,64,1,128]{3,1,2,0:T(8,128)S(1)}, f32[3,64,1,128]{3,1,2,0:T(8,128)S(1)}, u32[]{:S(2)}, u32[]{:S(2)}) collective-permute-start(f32[3,64,1,128]{3,1,2,0:T(8,128)S(1)} %bitcast.210), channel_id=1, source_target_pairs={{0,4},{4,8},{8,12},{12,16},{16,20},{20,24},{24,28},{1,5},{5,9},{9,... | collective-permute-start | bytes 294920 | tf_op jit(solution)/shard_map/ppermute | solution.py:22
  23.8 9.0 %collective-permute-start.31 = (f32[3,1,32,2]{2,3,1,0:T(2,128)S(1)}, f32[3,1,32,2]{2,3,1,0:T(2,128)S(1)}, u32[]{:S(2)}, u32[]{:S(2)}) collective-permute-start(f32[3,1,32,2]{2,3,1,0:T(2,128)S(1)} %pad_maximum_fusion.19), channel_id=1, source_target_pairs={{1,0},{2,1},{3,2},{5,4},{6,5},{7,6},{9,8},{10,9},{11,10},{13,12},{... | collective-permute-start | bytes 2312 | tf_op jit(solution)/shard_map/ppermute | solution.py:23
  27.8 8.7 %collective-permute-start.30 = (f32[3,1,32,2]{2,3,1,0:T(2,128)S(1)}, f32[3,1,32,2]{2,3,1,0:T(2,128)S(1)}, u32[]{:S(2)}, u32[]{:S(2)}) collective-permute-start(f32[3,1,32,2]{2,3,1,0:T(2,128)S(1)} %pad_maximum_fusion.19), channel_id=1, source_target_pairs={{0,1},{1,2},{2,3},{4,5},{5,6},{6,7},{8,9},{9,10},{10,11},{12,13},{... | collective-permute-start | bytes 2312 | tf_op jit(solution)/shard_map/ppermute | solution.py:22
  30.8 11.5 %collective-permute-start.19 = (f32[3,1,32,2]{2,3,1,0:T(2,128)S(1)}, f32[3,1,32,2]{2,3,1,0:T(2,128)S(1)}, u32[]{:S(2)}, u32[]{:S(2)}) collective-permute-start(f32[3,1,32,2]{2,3,1,0:T(2,128)S(1)} %pad_maximum_fusion.18), channel_id=1, source_target_pairs={{1,0},{2,1},{3,2},{5,4},{6,5},{7,6},{9,8},{10,9},{11,10},{13,12},{... | collective-permute-start | bytes 2312 | tf_op jit(solution)/shard_map/ppermute | solution.py:23
  32.8 9.6 %collective-permute-start.18 = (f32[3,1,32,2]{2,3,1,0:T(2,128)S(1)}, f32[3,1,32,2]{2,3,1,0:T(2,128)S(1)}, u32[]{:S(2)}, u32[]{:S(2)}) collective-permute-start(f32[3,1,32,2]{2,3,1,0:T(2,128)S(1)} %pad_maximum_fusion.18), channel_id=1, source_target_pairs={{0,1},{1,2},{2,3},{4,5},{5,6},{6,7},{8,9},{9,10},{10,11},{12,13},{... | collective-permute-start | bytes 2312 | tf_op jit(solution)/shard_map/ppermute | solution.py:22
  85.9 9.7 %collective-permute-start.7 = (f32[3,64,10,1]{1,2,3,0:T(8,128)S(1)}, f32[3,64,10,1]{1,2,3,0:T(8,128)S(1)}, u32[]{:S(2)}, u32[]{:S(2)}) collective-permute-start(f32[3,64,10,1]{1,2,3,0:T(8,128)S(1)} %get-tuple-element.147), channel_id=1, source_target_pairs={{1,0},{2,1},{3,2},{5,4},{6,5},{7,6},{9,8},{10,9},{11,10},{13,12},{... | collective-permute-start | bytes 23048 | tf_op jit(solution)/shard_map/ppermute | solution.py:23
  88.1 7.4 %collective-permute-start.6 = (f32[3,64,10,1]{1,2,3,0:T(8,128)S(1)}, f32[3,64,10,1]{1,2,3,0:T(8,128)S(1)}, u32[]{:S(2)}, u32[]{:S(2)}) collective-permute-start(f32[3,64,10,1]{1,2,3,0:T(8,128)S(1)} %get-tuple-element.146), channel_id=1, source_target_pairs={{0,1},{1,2},{2,3},{4,5},{5,6},{6,7},{8,9},{9,10},{10,11},{12,13},{... | collective-permute-start | bytes 23048 | tf_op jit(solution)/shard_map/ppermute | solution.py:22
  127.3 20.3 %collective-permute-start.9 = (f32[1,1,32,64]{3,2,1,0:T(8,128)S(1)}, f32[1,1,32,64]{3,2,1,0:T(8,128)S(1)}, u32[]{:S(2)}, u32[]{:S(2)}) collective-permute-start(f32[1,1,32,64]{3,2,1,0:T(8,128)S(1)} %fusion.47), channel_id=1, source_target_pairs={{4,0},{8,4},{12,8},{16,12},{20,16},{24,20},{28,24},{5,1},{9,5},{13... | collective-permute-start | bytes 24584 | tf_op jit(solution)/shard_map/ppermute | solution.py:23
  129.3 18.4 %collective-permute-start.8 = (f32[1,1,32,64]{3,2,1,0:T(8,128)S(1)}, f32[1,1,32,64]{3,2,1,0:T(8,128)S(1)}, u32[]{:S(2)}, u32[]{:S(2)}) collective-permute-start(f32[1,1,32,64]{3,2,1,0:T(8,128)S(1)} %fusion.47), channel_id=1, source_target_pairs={{0,4},{4,8},{8,12},{12,16},{16,20},{20,24},{24,28},{1,5},{5,9},{9,... | collective-permute-start | bytes 24584 | tf_op jit(solution)/shard_map/ppermute | solution.py:22
  132.6 9.2 %collective-permute-start.13 = (f32[1,1,32,64]{3,2,1,0:T(8,128)S(1)}, f32[1,1,32,64]{3,2,1,0:T(8,128)S(1)}, u32[]{:S(2)}, u32[]{:S(2)}) collective-permute-start(f32[1,1,32,64]{3,2,1,0:T(8,128)S(1)} %get-tuple-element.156), channel_id=1, source_target_pairs={{4,0},{8,4},{12,8},{16,12},{20,16},{24,20},{28,24},{5,1},{9,5},{13... | collective-permute-start | bytes 24584 | tf_op jit(solution)/shard_map/ppermute | solution.py:23
  141.9 11.6 %collective-permute-start.15 = (f32[3,1,32,64]{3,2,1,0:T(8,128)S(1)}, f32[3,1,32,64]{3,2,1,0:T(8,128)S(1)}, u32[]{:S(2)}, u32[]{:S(2)}) collective-permute-start(f32[3,1,32,64]{3,2,1,0:T(8,128)S(1)} %pad_maximum_fusion.7), channel_id=1, source_target_pairs={{1,0},{2,1},{3,2},{5,4},{6,5},{7,6},{9,8},{10,9},{11,10},{13,12},{... | collective-permute-start | bytes 73736 | tf_op jit(solution)/shard_map/ppermute | solution.py:23
  143.8 9.7 %collective-permute-start.14 = (f32[3,1,32,64]{3,2,1,0:T(8,128)S(1)}, f32[3,1,32,64]{3,2,1,0:T(8,128)S(1)}, u32[]{:S(2)}, u32[]{:S(2)}) collective-permute-start(f32[3,1,32,64]{3,2,1,0:T(8,128)S(1)} %pad_maximum_fusion.7), channel_id=1, source_target_pairs={{0,1},{1,2},{2,3},{4,5},{5,6},{6,7},{8,9},{9,10},{10,11},{12,13},{... | collective-permute-start | bytes 73736 | tf_op jit(solution)/shard_map/ppermute | solution.py:22
  147.7 9.2 %collective-permute-start.11 = (f32[3,1,32,64]{3,2,1,0:T(8,128)S(1)}, f32[3,1,32,64]{3,2,1,0:T(8,128)S(1)}, u32[]{:S(2)}, u32[]{:S(2)}) collective-permute-start(f32[3,1,32,64]{3,2,1,0:T(8,128)S(1)} %pad_maximum_fusion.6), channel_id=1, source_target_pairs={{1,0},{2,1},{3,2},{5,4},{6,5},{7,6},{9,8},{10,9},{11,10},{13,12},{... | collective-permute-start | bytes 73736 | tf_op jit(solution)/shard_map/ppermute | solution.py:23
  149.6 7.3 %collective-permute-start.10 = (f32[3,1,32,64]{3,2,1,0:T(8,128)S(1)}, f32[3,1,32,64]{3,2,1,0:T(8,128)S(1)}, u32[]{:S(2)}, u32[]{:S(2)}) collective-permute-start(f32[3,1,32,64]{3,2,1,0:T(8,128)S(1)} %pad_maximum_fusion.6), channel_id=1, source_target_pairs={{0,1},{1,2},{2,3},{4,5},{5,6},{6,7},{8,9},{9,10},{10,11},{12,13},{... | collective-permute-start | bytes 73736 | tf_op jit(solution)/shard_map/ppermute | solution.py:22
  161.0 21.1 %collective-permute-start.21 = (f32[1,1,32,64]{3,2,1,0:T(8,128)S(1)}, f32[1,1,32,64]{3,2,1,0:T(8,128)S(1)}, u32[]{:S(2)}, u32[]{:S(2)}) collective-permute-start(f32[1,1,32,64]{3,2,1,0:T(8,128)S(1)} %fusion.43), channel_id=1, source_target_pairs={{4,0},{8,4},{12,8},{16,12},{20,16},{24,20},{28,24},{5,1},{9,5},{13... | collective-permute-start | bytes 24584 | tf_op jit(solution)/shard_map/ppermute | solution.py:23
  164.6 17.6 %collective-permute-start.20 = (f32[1,1,32,64]{3,2,1,0:T(8,128)S(1)}, f32[1,1,32,64]{3,2,1,0:T(8,128)S(1)}, u32[]{:S(2)}, u32[]{:S(2)}) collective-permute-start(f32[1,1,32,64]{3,2,1,0:T(8,128)S(1)} %fusion.43), channel_id=1, source_target_pairs={{0,4},{4,8},{8,12},{12,16},{16,20},{20,24},{24,28},{1,5},{5,9},{9,... | collective-permute-start | bytes 24584 | tf_op jit(solution)/shard_map/ppermute | solution.py:22
  176.6 11.2 %collective-permute-start.27 = (f32[3,1,32,64]{3,2,1,0:T(8,128)S(1)}, f32[3,1,32,64]{3,2,1,0:T(8,128)S(1)}, u32[]{:S(2)}, u32[]{:S(2)}) collective-permute-start(f32[3,1,32,64]{3,2,1,0:T(8,128)S(1)} %pad_maximum_fusion.9), channel_id=1, source_target_pairs={{1,0},{2,1},{3,2},{5,4},{6,5},{7,6},{9,8},{10,9},{11,10},{13,12},{... | collective-permute-start | bytes 73736 | tf_op jit(solution)/shard_map/ppermute | solution.py:23
  178.9 8.8 %collective-permute-start.26 = (f32[3,1,32,64]{3,2,1,0:T(8,128)S(1)}, f32[3,1,32,64]{3,2,1,0:T(8,128)S(1)}, u32[]{:S(2)}, u32[]{:S(2)}) collective-permute-start(f32[3,1,32,64]{3,2,1,0:T(8,128)S(1)} %pad_maximum_fusion.9), channel_id=1, source_target_pairs={{0,1},{1,2},{2,3},{4,5},{5,6},{6,7},{8,9},{9,10},{10,11},{12,13},{... | collective-permute-start | bytes 73736 | tf_op jit(solution)/shard_map/ppermute | solution.py:22
  182.2 9.0 %collective-permute-start.23 = (f32[3,1,32,64]{3,2,1,0:T(8,128)S(1)}, f32[3,1,32,64]{3,2,1,0:T(8,128)S(1)}, u32[]{:S(2)}, u32[]{:S(2)}) collective-permute-start(f32[3,1,32,64]{3,2,1,0:T(8,128)S(1)} %pad_maximum_fusion.8), channel_id=1, source_target_pairs={{1,0},{2,1},{3,2},{5,4},{6,5},{7,6},{9,8},{10,9},{11,10},{13,12},{... | collective-permute-start | bytes 73736 | tf_op jit(solution)/shard_map/ppermute | solution.py:23
  (27 other events, 209.4 us)
where the time goes:
time: 196 us; the launch traced here: 195 us
  starting transfers between devices  94.4 us (48%)
  local copies, waits for them, and re-layouts  57.2 us (29%)
  other arithmetic  21 us (11%)
  matrix products  12.3 us (6%)
  waiting for transfers between devices  8.99 us (5%)
    ppermute x16, starting transfers between devices, extended(): before = lax.ppermute(last, axis, up)  48.3 us
    ppermute x16, starting transfers between devices, extended(): after = lax.ppermute(first, axis, down)  46.1 us
    scatter x2, local copies, waits for them, and re-layouts, walls(): padded.at[..., :rim_width, :]  22 us
    scatter x2, local copies, waits for them, and re-layouts, walls(): padded.at[..., -rim_width:, :]  22 us
    ppermute x16, waiting for transfers between devices, extended(): before = lax.ppermute(last, axis, up)  8.95 us
    dot_general x2, matrix products, increments(): jnp.einsum('fmp,gm->fpg', centered, obs_anom, precision=lax.Precision.HIG...  6.65 us
    dot_general x2, matrix products, increments(): jnp.einsum('fpg,gm->fmp', covariance * taper_weight[None], obs_weight, pr...  5.64 us
    div x8, other arithmetic, hll_flux(): return numer / (fast_wave - slow_wave)[None]  5.56 us
  transfers between devices with their start and end apart: 32, of which 3 were waited for; matrix products, arithmetic and copies ran while one was open for 10% of the time, Pallas kernels for 0%

commit v1 on v0

v1 whole, which is shorter than its diff:
```python
import functools

import jax
import jax.numpy as jnp
from jax import lax
from jax.experimental import pallas as pl
from jax.experimental.pallas import tpu as pltpu
from jax.sharding import PartitionSpec as P

LOC = 6
GRAVITY = 9.81
SPACING = 2.0
STEP = 0.08
F32 = jnp.float32
BF16 = jnp.bfloat16
MESH = pl.DeviceIdType.MESH

TILES = [(dr, dc) for dc in (0, -1, 1) for dr in (-1, 0, 1)]
OWN = 1


def cell(h, n, t, vn, c):
    return (h, n, t, vn, vn - c, vn + c, (0.5 * GRAVITY) * h * h)


def face(lo, up):
    slow = jnp.minimum(jnp.minimum(lo[4], up[4]), 0.0)
    fast = jnp.maximum(jnp.maximum(lo[5], up[5]), 0.0)
    inv = 1.0 / (fast - slow)
    a = fast * inv
    b = slow * inv
    wl = a * (lo[3] - slow)
    wu = b * (fast - up[3])
    return (
        wl * lo[0] + wu * up[0],
        wl * lo[1] + wu * up[1] + (a * lo[6] - b * up[6]),
        wl * lo[2] + wu * up[2],
    )


def split2(x):
    hi = x.astype(BF16)
    return hi, (x - hi.astype(F32)).astype(BF16)


def kernel(
    x_ref, cells_ref, count_ref, value_ref, noise_ref, var_ref, out_ref,
    S, SEC, C, GR, OWNP, GC, META, PK, TC, TE, OH, OBS, RC, RE, INCE,
    row_send, row_recv, col_send, col_recv, meta_send, meta_recv, pk_send, pk_recv,
):
    n_row, n_col = lax.axis_size("row"), lax.axis_size("col")
    my_r, my_c = lax.axis_index("row"), lax.axis_index("col")
    rows, members, lanes = S.shape[1:]
    batches, slots = cells_ref.shape
    at_top, at_bottom = my_r == 0, my_r == n_row - 1
    at_left, at_right = my_c == 0, my_c == n_col - 1
    blocks = members // 8

    def present(dr, dc):
        ok = None
        for cond, d in ((my_r > 0, dr == -1), (my_r < n_row - 1, dr == 1),
                        (my_c > 0, dc == -1), (my_c < n_col - 1, dc == 1)):
            if d:
                ok = cond if ok is None else jnp.logical_and(ok, cond)
        return ok

    def device(dr, dc):
        return (jnp.clip(my_r + dr, 0, n_row - 1), jnp.clip(my_c + dc, 0, n_col - 1))

    others = [(k, dr, dc) for k, (dr, dc) in enumerate(TILES) if k != OWN]

    def mirror(k):
        dr, dc = TILES[k]
        return TILES.index((-dr, -dc))

    barrier = pltpu.get_barrier_semaphore()
    for k, dr, dc in others:
        @pl.when(present(dr, dc))
        def _(dr=dr, dc=dc):
            pl.semaphore_signal(barrier, inc=1, device_id=device(dr, dc), device_id_type=MESH)

    for r in (0, rows - 1) + tuple(range(1, rows - 1)):
        for f in range(3):
            S[f, r] = x_ref[f, pl.ds(r, members, stride=rows), :]

    near_r = 1 + (my_r > 0).astype(jnp.int32) + (my_r < n_row - 1).astype(jnp.int32)
    near_c = 1 + (my_c > 0).astype(jnp.int32) + (my_c < n_col - 1).astype(jnp.int32)
    pl.semaphore_wait(barrier, near_r * near_c - 1)

    def row_copies(stage, src):
        up = pltpu.make_async_remote_copy(
            src_ref=src.at[:, 0], dst_ref=GR.at[stage, 1],
            send_sem=row_send.at[stage, 0], recv_sem=row_recv.at[stage, 1],
            device_id=device(-1, 0), device_id_type=MESH)
        down = pltpu.make_async_remote_copy(
            src_ref=src.at[:, rows - 1], dst_ref=GR.at[stage, 0],
            send_sem=row_send.at[stage, 1], recv_sem=row_recv.at[stage, 0],
            device_id=device(1, 0), device_id_type=MESH)
        return up, down

    def row_start(stage, src):
        up, down = row_copies(stage, src)
        pl.when(my_r > 0)(up.start)
        pl.when(my_r < n_row - 1)(down.start)
        for side, r, wall in ((0, 0, at_top), (1, rows - 1, at_bottom)):
            @pl.when(wall)
            def _(side=side, r=r):
                GR[stage, side, 0] = src[0, r]
                GR[stage, side, 1] = src[1, r]
                GR[stage, side, 2] = -src[2, r]

    def row_wait(stage, src):
        up, down = row_copies(stage, src)

        @pl.when(my_r > 0)
        def _():
            up.wait_send()
            down_like = pltpu.make_async_remote_copy(
                src_ref=src.at[:, rows - 1], dst_ref=GR.at[stage, 0],
                send_sem=row_send.at[stage, 1], recv_sem=row_recv.at[stage, 0],
                device_id=device(-1, 0), device_id_type=MESH)
            down_like.wait_recv()

        @pl.when(my_r < n_row - 1)
        def _():
            down.wait_send()
            up_like = pltpu.make_async_remote_copy(
                src_ref=src.at[:, 0], dst_ref=GR.at[stage, 1],
                send_sem=row_send.at[stage, 0], recv_sem=row_recv.at[stage, 1],
                device_id=device(1, 0), device_id_type=MESH)
            up_like.wait_recv()

    def col_copies(stage):
        left = pltpu.make_async_remote_copy(
            src_ref=OWNP.at[stage], dst_ref=GC.at[stage, 1],
            send_sem=col_send.at[stage, 0], recv_sem=col_recv.at[stage, 1],
            device_id=device(0, -1), device_id_type=MESH)
        right = pltpu.make_async_remote_copy(
            src_ref=OWNP.at[stage], dst_ref=GC.at[stage, 0],
            send_sem=col_send.at[stage, 1], recv_sem=col_recv.at[stage, 0],
            device_id=device(0, 1), device_id_type=MESH)
        return left, right

    lane8 = lax.broadcasted_iota(jnp.int32, (8, lanes), 1)
    lane64 = lax.broadcasted_iota(jnp.int32, (members, lanes), 1)

    def col_start(stage, src):
        def pack(i, carry):
            m = pl.ds(pl.multiple_of(i * 8, 8), 8)
            packed = jnp.zeros((8, lanes), F32)
            for f in range(3):
                for r in range(rows):
                    k = f * rows + r
                    rolled = pltpu.roll(src[f, r, m, :], 2 * k + 1, 1)
                    packed = jnp.where(lane8 // 2 == k, rolled, packed)
            OWNP[stage, m, :] = packed
            return carry

        lax.fori_loop(0, blocks, pack, 0)
        left, right = col_copies(stage)
        pl.when(my_c > 0)(left.start)
        pl.when(my_c < n_col - 1)(right.start)
        flip = jnp.where((lane64 >= 2 * rows) & (lane64 < 4 * rows), -1.0, 1.0)

        @pl.when(at_left)
        def _():
            GC[stage, 0] = pltpu.roll(OWNP[stage], lanes - 1, 1) * flip

        @pl.when(at_right)
        def _():
            GC[stage, 1] = pltpu.roll(OWNP[stage], 1, 1) * flip

    def col_wait(stage):
        left, right = col_copies(stage)

        @pl.when(my_c > 0)
        def _():
            left.wait_send()
            right.wait_recv()

        @pl.when(my_c < n_col - 1)
        def _():
            right.wait_send()
            left.wait_recv()

    def advance(stage, src, first, last, finish):
        def body(i, carry):
            m = pl.ds(pl.multiple_of(i * 8, 8), 8)
            even = lane8 % 2 == 0
            own = OWNP[stage, m, :]
            lo = jnp.where(even, own, pltpu.roll(GC[stage, 0, m, :], 1, 1))
            up = jnp.where(even, pltpu.roll(GC[stage, 1, m, :], lanes - 1, 1), own)

            def unpack(v):
                h, n, t = v, pltpu.roll(v, lanes - 2 * rows, 1), pltpu.roll(v, lanes - 4 * rows, 1)
                return cell(h, n, t, n / h, jnp.sqrt(GRAVITY * h))

            edge = face(unpack(lo), unpack(up))

            def load(r):
                if r < 0:
                    f = [GR[stage, 0, f, m, :] for f in range(3)]
                elif r >= rows:
                    f = [GR[stage, 1, f, m, :] for f in range(3)]
                else:
                    f = [src[f, r, m, :] for f in range(3)]
                return f

            def derive(f):
                rec = 1.0 / f[0]
                return f[1] * rec, f[2] * rec, jnp.sqrt(GRAVITY * f[0])

            def rowcell(f, d):
                return cell(f[0], f[2], f[1], d[1], d[2])

            fb = load(first - 1)
            fc = load(first)
            dc = derive(fc)
            below = face(rowcell(fb, derive(fb)), rowcell(fc, dc))
            for r in range(first, last):
                fn = load(r + 1)
                dn = derive(fn)
                above = face(rowcell(fc, dc), rowcell(fn, dn))
                left = [pltpu.roll(v, 1, 1) for v in (*fc, dc[0], dc[2])]
                flux = face(cell(*left), cell(*fc, dc[0], dc[2]))
                out = []
                for f, g in ((0, 0), (1, 2), (2, 1)):
                    q = pltpu.roll(edge[f], lanes - 1 - 2 * r, 1)
                    low = jnp.where(lane8 == 0, q, flux[f])
                    high = jnp.where(lane8 == lanes - 1, q, pltpu.roll(low, lanes - 1, 1))
                    out.append((high - low + above[g] - below[g]) * (-1.0 / SPACING))
                finish(r, m, fc, out)
                fc, dc, below = fn, dn, above
            return carry

        lax.fori_loop(0, blocks, body, 0)

    def finish1(r, m, fields, tend):
        for f in range(3):
            SEC[f, r, m, :] = fields[f] + STEP * tend[f]

    def finish2(r, m, fields, tend):
        for f in range(3):
            C[f, r, m, :] = 0.5 * (S[f, r, m, :] + fields[f] + STEP * tend[f])

    row_start(0, S)
    META[OWN] = jnp.zeros((8, lanes), F32)
    META[OWN, 0:batches, 0:slots] = cells_ref[...].astype(F32)
    col_start(0, S)

    def meta_copy(k, dr, dc):
        return pltpu.make_async_remote_copy(
            src_ref=META.at[OWN], dst_ref=META.at[mirror(k)],
            send_sem=meta_send.at[k], recv_sem=meta_recv.at[mirror(k)],
            device_id=device(dr, dc), device_id_type=MESH)

    def pk_copy(b, k, dr, dc):
        return pltpu.make_async_remote_copy(
            src_ref=PK.at[b, OWN], dst_ref=PK.at[b, mirror(k)],
            send_sem=pk_send.at[b, k], recv_sem=pk_recv.at[b, mirror(k)],
            device_id=device(dr, dc), device_id_type=MESH)

    for k, dr, dc in others:
        @pl.when(present(dr, dc))
        def _(k=k, dr=dr, dc=dc):
            meta_copy(k, dr, dc).start()

        @pl.when(jnp.logical_not(present(dr, dc)))
        def _(k=k):
            META[k] = jnp.zeros((8, lanes), F32)
            for b in range(batches):
                PK[b, k] = jnp.zeros((slots, lanes), F32)

    eye = lax.broadcasted_iota(jnp.int32, (slots, lanes), 0) == lax.broadcasted_iota(
        jnp.int32, (slots, lanes), 1)

    def column(row):
        return jnp.sum(jnp.where(eye, row, 0.0), axis=1, keepdims=True)

    lane_s = lax.broadcasted_iota(jnp.int32, (slots, lanes), 1).astype(F32)
    wide = lambda row: jnp.concatenate([row, jnp.zeros((1, lanes - slots), F32)], axis=1)
    for b in range(batches):
        own_cell = column(META[OWN, b:b + 1, :])
        for r in range(rows):
            OH[b, :, r * lanes:(r + 1) * lanes] = jnp.where(
                own_cell == lane_s + float(r * lanes), 1.0, 0.0).astype(BF16)
        OBS[b, 0] = jnp.broadcast_to(column(wide(value_ref[b:b + 1, :])), (slots, lanes))
        OBS[b, 1] = jnp.broadcast_to(column(wide(var_ref[b:b + 1, :])), (slots, lanes))

    col_wait(0)
    advance(0, S, 1, rows - 1, finish1)
    row_wait(0, S)
    advance(0, S, 0, 1, finish1)
    advance(0, S, rows - 1, rows, finish1)

    row_start(1, SEC)
    col_start(1, SEC)

    for k, dr, dc in others:
        @pl.when(present(dr, dc))
        def _(k=k, dr=dr, dc=dc):
            meta_copy(k, dr, dc).wait_send()
            meta_copy(mirror(k), -dr, -dc).wait_recv()

    window = 2 * LOC
    members_1 = float(members - 1)
    lane_1 = lax.broadcasted_iota(jnp.int32, (1, lanes), 1)
    in_window = lane_1 % window
    edge_row = (lane_1 // window).astype(F32)
    edge_col = jnp.where(in_window < LOC, lanes - LOC + in_window, in_window - LOC).astype(F32)
    inv_loc = 1.0 / (LOC * LOC)
    for b in range(batches):
        for k, (dr, dc) in enumerate(TILES):
            at = column(META[k, b:b + 1, :])
            g_row = jnp.floor(at * (1.0 / lanes))
            g_col = at - g_row * lanes + float(dc * lanes)
            g_row = g_row + float(dr * rows)
            where = pl.ds((k % 3) * slots, slots)
            if dc == 0:
                dcol = lane_s - g_col
                dcol = dcol * dcol
                for r in range(rows):
                    drow = float(r) - g_row
                    t = jnp.maximum(1.0 - (dcol + drow * drow) * inv_loc, 0.0)
                    TC[b, where, r * lanes:(r + 1) * lanes] = t * t * (1.0 / members_1)
            else:
                dcol = edge_col - g_col
                drow = edge_row - g_row
                t = jnp.maximum(1.0 - (dcol * dcol + drow * drow) * inv_loc, 0.0)
                TE[b, (k - 3) * slots:(k - 2) * slots, :] = t * t * (1.0 / members_1)

    col_wait(1)
    advance(1, SEC, 1, rows - 1, finish2)
    row_wait(1, SEC)
    advance(1, SEC, 0, 1, finish2)
    advance(1, SEC, rows - 1, rows, finish2)

    dot = functools.partial(lax.dot_general, preferred_element_type=F32)
    nn = (((1,), (0,)), ((), ()))
    nt = (((1,), (1,)), ((), ()))

    def operands(packets):
        lane = lax.broadcasted_iota(jnp.int32, packets.shape, 1)
        swapped = pltpu.roll(packets, lanes // 2, 1)
        anom = jnp.where(lane < members, packets, swapped)
        weight = jnp.where(lane < members, swapped, packets)
        hi, lo = split2(anom)
        w_hi = weight.astype(BF16).astype(F32)
        w = jnp.where(lane < members, w_hi, weight - w_hi)
        return (jnp.concatenate([hi, lo], axis=1),
                jnp.concatenate([w, w], axis=0).T.astype(BF16))

    def increment(anom, weight, centred, taper):
        cov = dot(anom, centred, nn) * taper
        hi, lo = split2(cov)
        both = dot(weight, jnp.concatenate([hi, lo], axis=0), nn)
        return both[:members] + both[members:]

    def centre(v):
        hi, lo = split2(v - jnp.mean(v, axis=0, keepdims=True))
        return jnp.concatenate([hi, lo, hi, lo], axis=0)

    for b in range(batches):
        depth = jnp.concatenate([C[0, r] for r in range(rows)], axis=1)
        hi, rest = depth.astype(BF16), None
        rest = depth - hi.astype(F32)
        mid, low = split2(rest)
        onehot = OH[b]
        prior = dot(onehot, hi, nt) + (dot(onehot, mid, nt) + dot(onehot, low, nt))
        anom = prior - jnp.mean(prior, axis=1, keepdims=True)
        spread = jnp.sum(anom * anom, axis=1, keepdims=True) * (1.0 / members_1)
        slot = lax.broadcasted_iota(jnp.int32, (slots, members), 0)
        live = jnp.where(slot < count_ref[0, 0, b], 1.0, 0.0)
        weight = live * (OBS[b, 0, :, :members] + noise_ref[b] - prior) / (
            spread + OBS[b, 1, :, :members])
        PK[b, OWN] = jnp.concatenate([anom, weight], axis=1)
        for k, dr, dc in others:
            @pl.when(present(dr, dc))
            def _(k=k, dr=dr, dc=dc):
                pk_copy(b, k, dr, dc).start()

        def prepare(f, carry):
            edges = jnp.zeros((members, lanes), F32)
            for r in range(rows):
                rolled = pltpu.roll(C[f, r], window * r + LOC, 1)
                edges = jnp.where(lane64 // window == r, rolled, edges)
            RE[f] = centre(edges)
            for pair in range(rows // 2):
                v = jnp.concatenate([C[f, 2 * pair], C[f, 2 * pair + 1]], axis=1)
                RC[f, pair] = centre(v)
            return carry

        lax.fori_loop(0, 3, prepare, 0)

        def arrive(ks):
            for k, dr, dc in others:
                if k in ks:
                    @pl.when(present(dr, dc))
                    def _(k=k, dr=dr, dc=dc):
                        pk_copy(b, k, dr, dc).wait_send()
                        pk_copy(b, mirror(k), -dr, -dc).wait_recv()

        arrive((0, 2))
        anom_c, weight_c = operands(PK[b, 0:3].reshape(3 * slots, lanes))

        def update(f, carry):
            for pair in range(rows // 2):
                span = slice(2 * pair * lanes, (2 * pair + 2) * lanes)
                inc = increment(anom_c, weight_c, RC[f, pair], TC[b, :, span])
                C[f, 2 * pair] = C[f, 2 * pair] + inc[:, :lanes]
                C[f, 2 * pair + 1] = C[f, 2 * pair + 1] + inc[:, lanes:]
            return carry

        lax.fori_loop(0, 3, update, 0)
        arrive((3, 4, 5, 6, 7, 8))
        anom_e, weight_e = operands(PK[b, 3:9].reshape(6 * slots, lanes))

        def update_edges(f, carry):
            inc = increment(anom_e, weight_e, RE[f], TE[b])
            outer = (lane64 < LOC) | (lane64 >= lanes - LOC)
            for r in range(rows):
                back = pltpu.roll(inc, (lanes - (window * r + LOC)) % lanes, 1)
                done = C[f, r] + jnp.where(outer, back, 0.0)
                if b < batches - 1:
                    C[f, r] = done
                else:
                    out_ref[f, pl.ds(r, members, stride=rows), :] = done
            return carry

        lax.fori_loop(0, 3, update_edges, 0)


def body(state, gauge_cells, gauge_count, obs_value, obs_noise, obs_var):
    fields, members, rows, lanes = state.shape
    batches, slots = gauge_cells.shape[2:]
    vmem = pl.BlockSpec(memory_space=pltpu.VMEM)
    dma = pltpu.SemaphoreType.DMA
    grid = (fields, rows, members, lanes)
    out = pl.pallas_call(
        kernel,
        out_shape=jax.ShapeDtypeStruct((fields, members * rows, lanes), F32),
        in_specs=[vmem, vmem, pl.BlockSpec(memory_space=pltpu.SMEM), vmem, vmem, vmem],
        out_specs=vmem,
        scratch_shapes=[
            pltpu.VMEM(grid, F32),
            pltpu.VMEM(grid, F32),
            pltpu.VMEM(grid, F32),
            pltpu.VMEM((2, 2, fields, members, lanes), F32),
            pltpu.VMEM((2, members, lanes), F32),
            pltpu.VMEM((2, 2, members, lanes), F32),
            pltpu.VMEM((9, 8, lanes), F32),
            pltpu.VMEM((batches, 9, slots, lanes), F32),
            pltpu.VMEM((batches, 3 * slots, rows * lanes), F32),
            pltpu.VMEM((batches, 6 * slots, lanes), F32),
            pltpu.VMEM((batches, slots, rows * lanes), BF16),
            pltpu.VMEM((batches, 2, slots, lanes), F32),
            pltpu.VMEM((fields, rows // 2, 4 * members, 2 * lanes), BF16),
            pltpu.VMEM((fields, 4 * members, lanes), BF16),
            pltpu.VMEM((fields, members, lanes), F32),
            dma((2, 2)), dma((2, 2)), dma((2, 2)), dma((2, 2)),
            dma((9,)), dma((9,)), dma((batches, 9)), dma((batches, 9)),
        ],
        compiler_params=pltpu.CompilerParams(
            collective_id=0, has_side_effects=True, vmem_limit_bytes=40 * 1024 * 1024),
    )(
        state.reshape(fields, members * rows, lanes),
        gauge_cells.reshape(batches, slots),
        gauge_count,
        obs_value.reshape(batches, slots),
        obs_noise.reshape(batches, slots, members),
        obs_var.reshape(batches, slots),
    )
    return out.reshape(state.shape)


def solution(mesh):
    placed = (
        P(None, None, "row", "col"),
        P("row", "col", None, None),
        P("row", "col", None),
        P("row", "col", None, None),
        P("row", "col", None, None, None),
        P("row", "col", None, None),
    )
    return jax.shard_map(
        body, mesh=mesh, in_specs=placed, out_specs=P(None, None, "row", "col"), check_vma=False
    )
```

time: 196 us -> 47.4 us (0.24)
  the two profiles are of different devices: /device:TPU:17 before, /device:TPU:0 now
where the time goes in v1:
time: 47.4 us; the launch traced here: 47.2 us
  Pallas kernels  43.7 us (92%)
  local copies, waits for them, and re-layouts  3.48 us (7%)
    pallas_call x1, Pallas kernels, body(): pl.pallas_call(kernel, out_shape=jax.ShapeDtypeStruct((fields, members *...  43.7 us
    unnamed x13, local copies, waits for them, and re-layouts  3.48 us

profile of v1, /device:TPU:0, one launch (start us, length us, event | category | flops | bytes accessed | tf_op | source)
XLA Modules:
  0.0 47.2 jit_solution(16113076267031235304)
XLA Ops:
  0.0 0.0 copy-start.3
  0.0 0.0 copy-start.4
  0.0 0.0 copy-start.2
  0.0 0.0 copy-start.5
  0.0 0.7 %copy-done.3 = f32[1,1,2,32]{3,2,1,0:T(2,128)S(1)} copy-done((f32[1,1,2,32]{3,2,1,0:T(2,128)S(1)}, f32[1,1,2,32]{3,2,1,0:T(2,128)}, u32[]{:S(2)}) %copy-start.3) | copy-done | bytes 280
  0.7 0.0 copy-done.4
  0.7 0.0 copy-done.2
  0.7 0.0 copy-done.5
  0.7 0.0 copy-start
  0.7 1.1 %copy-done = f32[3,64,8,128]{3,2,1,0:T(8,128)S(1)} copy-done((f32[3,64,8,128]{3,2,1,0:T(8,128)S(1)}, f32[3,64,8,128]{3,2,1,0:T(8,128)}, u32[]{:S(2)}) %copy-start) | copy-done | bytes 786456
  1.8 0.0 copy-start.1
  1.9 0.8 %copy-done.1 = f32[1,1,2,32,64]{4,3,2,1,0:T(8,128)S(1)} copy-done((f32[1,1,2,32,64]{4,3,2,1,0:T(8,128)S(1)}, f32[1,1,2,32,64]{4,3,2,1,0:T(8,128)}, u32[]{:S(2)}) %copy-start.1) | copy-done | bytes 16408
  2.6 43.7 %shard_map.64 = f32[3,512,128]{2,1,0:T(8,128)S(1)} custom-call(f32[3,512,128]{2,1,0:T(8,128)S(1)} %bitcast.7, s32[2,32]{1,0:T(2,128)S(1)} %bitcast.9, s32[1,1,2]{2,1,0:T(1,128)S(1)} %copy-done.5, f32[2,32]{1,0:T(2,128)S(1)} %bitcast.10, f32[2,32,64]{2,1,0:T(8,128)S(1)} %bitcast.8, f32[2,32]{1,0:T(2,128)S(1)} %bitcast.11), custom_call_target="tpu_custom_call" | custom-call | tf_op jit(solution)/shard_map/pallas_call | solution.py:439
  46.3 0.9 %copy.8 = f32[3,64,8,128]{3,2,1,0:T(8,128)} copy(f32[3,64,8,128]{3,2,1,0:T(8,128)S(1)} %bitcast.6) | data formatting | bytes 1572864
Async XLA Ops:
  0.0 0.7 %copy-start.3 = (f32[1,1,2,32]{3,2,1,0:T(2,128)S(1)}, f32[1,1,2,32]{3,2,1,0:T(2,128)}, u32[]{:S(2)}) copy-start(f32[1,1,2,32]{3,2,1,0:T(2,128)} %param.9) | copy-start | bytes 772
  0.0 0.7 %copy-start.4 = (f32[1,1,2,32]{3,2,1,0:T(2,128)S(1)}, f32[1,1,2,32]{3,2,1,0:T(2,128)}, u32[]{:S(2)}) copy-start(f32[1,1,2,32]{3,2,1,0:T(2,128)} %param.11) | copy-start | bytes 772
  0.0 0.7 %copy-start.2 = (s32[1,1,2,32]{3,2,1,0:T(2,128)S(1)}, s32[1,1,2,32]{3,2,1,0:T(2,128)}, u32[]{:S(2)}) copy-start(s32[1,1,2,32]{3,2,1,0:T(2,128)} %param.7) | copy-start | bytes 772
  0.0 0.7 %copy-start.5 = (s32[1,1,2]{2,1,0:T(1,128)S(1)}, s32[1,1,2]{2,1,0:T(1,128)}, u32[]{:S(2)}) copy-start(s32[1,1,2]{2,1,0:T(1,128)} %count_ref.1) | copy-start | bytes 28
  0.7 1.1 %copy-start = (f32[3,64,8,128]{3,2,1,0:T(8,128)S(1)}, f32[3,64,8,128]{3,2,1,0:T(8,128)}, u32[]{:S(2)}) copy-start(f32[3,64,8,128]{3,2,1,0:T(8,128)} %param.6) | copy-start | bytes 2359300
  1.8 0.8 %copy-start.1 = (f32[1,1,2,32,64]{4,3,2,1,0:T(8,128)S(1)}, f32[1,1,2,32,64]{4,3,2,1,0:T(8,128)}, u32[]{:S(2)}) copy-start(f32[1,1,2,32,64]{4,3,2,1,0:T(8,128)} %param.10) | copy-start | bytes 49156

commit v2 on v1

--- a/solution.py
+++ b/solution.py
@@ -11,6 +11,9 @@
 GRAVITY = 9.81
 SPACING = 2.0
 STEP = 0.08
+ROOT_G = GRAVITY ** 0.5
+INNER = 16
+OUTER = 32
 F32 = jnp.float32
 BF16 = jnp.bfloat16
 MESH = pl.DeviceIdType.MESH
@@ -44,9 +47,10 @@
 
 
 def kernel(
-    x_ref, cells_ref, count_ref, value_ref, noise_ref, var_ref, out_ref,
-    S, SEC, C, GR, OWNP, GC, META, PK, TC, TE, OH, OBS, RC, RE, INCE,
-    row_send, row_recv, col_send, col_recv, meta_send, meta_recv, pk_send, pk_recv,
+    x_hbm, cells_hbm, count_ref, value_hbm, noise_hbm, var_hbm, out_ref,
+    x_ref, cells_ref, value_ref, noise_ref, var_ref,
+    S, SEC, C, GR, OWNP, GC, META, PK, TC, TE, OH, OBS, RC, RE, EF,
+    in_sem, row_send, row_recv, col_send, col_recv, meta_send, meta_recv, pk_send, pk_recv,
 ):
     n_row, n_col = lax.axis_size("row"), lax.axis_size("col")
     my_r, my_c = lax.axis_index("row"), lax.axis_index("col")
@@ -73,12 +77,20 @@
         dr, dc = TILES[k]
         return TILES.index((-dr, -dc))
 
+    loads = [
+        pltpu.make_async_copy(a, b, in_sem.at[i]) for i, (a, b) in enumerate((
+            (x_hbm, x_ref), (cells_hbm, cells_ref), (value_hbm, value_ref),
+            (noise_hbm, noise_ref), (var_hbm, var_ref)))]
+    for load in loads:
+        load.start()
+
     barrier = pltpu.get_barrier_semaphore()
     for k, dr, dc in others:
         @pl.when(present(dr, dc))
         def _(dr=dr, dc=dc):
             pl.semaphore_signal(barrier, inc=1, device_id=device(dr, dc), device_id_type=MESH)
 
+    loads[0].wait()
     for r in (0, rows - 1) + tuple(range(1, rows - 1)):
         for f in range(3):
             S[f, r] = x_ref[f, pl.ds(r, members, stride=rows), :]
@@ -142,21 +154,22 @@
         return left, right
 
     lane8 = lax.broadcasted_iota(jnp.int32, (8, lanes), 1)
+    lane32 = lax.broadcasted_iota(jnp.int32, (32, lanes), 1)
     lane64 = lax.broadcasted_iota(jnp.int32, (members, lanes), 1)
 
     def col_start(stage, src):
         def pack(i, carry):
-            m = pl.ds(pl.multiple_of(i * 8, 8), 8)
-            packed = jnp.zeros((8, lanes), F32)
+            m = pl.ds(pl.multiple_of(i * 32, 8), 32)
+            packed = jnp.zeros((32, lanes), F32)
             for f in range(3):
                 for r in range(rows):
                     k = f * rows + r
                     rolled = pltpu.roll(src[f, r, m, :], 2 * k + 1, 1)
-                    packed = jnp.where(lane8 // 2 == k, rolled, packed)
+                    packed = jnp.where(lane32 // 2 == k, rolled, packed)
             OWNP[stage, m, :] = packed
             return carry
 
-        lax.fori_loop(0, blocks, pack, 0)
+        lax.fori_loop(0, members // 32, pack, 0)
         left, right = col_copies(stage)
         pl.when(my_c > 0)(left.start)
         pl.when(my_c < n_col - 1)(right.start)
@@ -183,19 +196,33 @@
             right.wait_send()
             left.wait_recv()
 
-    def advance(stage, src, first, last, finish):
+    def edge_flux(stage):
+        even = lax.broadcasted_iota(jnp.int32, (32, lanes), 1) % 2 == 0
+
         def body(i, carry):
-            m = pl.ds(pl.multiple_of(i * 8, 8), 8)
-            even = lane8 % 2 == 0
+            m = pl.ds(pl.multiple_of(i * 32, 8), 32)
             own = OWNP[stage, m, :]
             lo = jnp.where(even, own, pltpu.roll(GC[stage, 0, m, :], 1, 1))
             up = jnp.where(even, pltpu.roll(GC[stage, 1, m, :], lanes - 1, 1), own)
 
             def unpack(v):
                 h, n, t = v, pltpu.roll(v, lanes - 2 * rows, 1), pltpu.roll(v, lanes - 4 * rows, 1)
-                return cell(h, n, t, n / h, jnp.sqrt(GRAVITY * h))
-
-            edge = face(unpack(lo), unpack(up))
+                rs = lax.rsqrt(h)
+                return cell(h, n, t, n * (rs * rs), ROOT_G * (h * rs))
+
+            done = face(unpack(lo), unpack(up))
+            for f in range(3):
+                EF[f, m, :] = done[f]
+            return carry
+
+        lax.fori_loop(0, members // 32, body, 0)
+
+    def advance(stage, src, tall, spans, finish):
+        lane_b = lax.broadcasted_iota(jnp.int32, (tall, lanes), 1)
+
+        def body(i, carry):
+            m = pl.ds(pl.multiple_of(i * tall, 8), tall)
+            edge = [EF[f, m, :] for f in range(3)]
 
             def load(r):
                 if r < 0:
@@ -207,33 +234,35 @@
                 return f
 
             def derive(f):
-                rec = 1.0 / f[0]
-                return f[1] * rec, f[2] * rec, jnp.sqrt(GRAVITY * f[0])
+                rs = lax.rsqrt(f[0])
+                rec = rs * rs
+                return f[1] * rec, f[2] * rec, ROOT_G * (f[0] * rs)
 
             def rowcell(f, d):
                 return cell(f[0], f[2], f[1], d[1], d[2])
 
-            fb = load(first - 1)
-            fc = load(first)
-            dc = derive(fc)
-            below = face(rowcell(fb, derive(fb)), rowcell(fc, dc))
-            for r in range(first, last):
-                fn = load(r + 1)
-                dn = derive(fn)
-                above = face(rowcell(fc, dc), rowcell(fn, dn))
-                left = [pltpu.roll(v, 1, 1) for v in (*fc, dc[0], dc[2])]
-                flux = face(cell(*left), cell(*fc, dc[0], dc[2]))
-                out = []
-                for f, g in ((0, 0), (1, 2), (2, 1)):
-                    q = pltpu.roll(edge[f], lanes - 1 - 2 * r, 1)
-                    low = jnp.where(lane8 == 0, q, flux[f])
-                    high = jnp.where(lane8 == lanes - 1, q, pltpu.roll(low, lanes - 1, 1))
-                    out.append((high - low + above[g] - below[g]) * (-1.0 / SPACING))
-                finish(r, m, fc, out)
-                fc, dc, below = fn, dn, above
+            for first, last in spans:
+                fb = load(first - 1)
+                fc = load(first)
+                dc = derive(fc)
+                below = face(rowcell(fb, derive(fb)), rowcell(fc, dc))
+                for r in range(first, last):
+                    fn = load(r + 1)
+                    dn = derive(fn)
+                    above = face(rowcell(fc, dc), rowcell(fn, dn))
+                    left = [pltpu.roll(v, 1, 1) for v in (*fc, dc[0], dc[2])]
+                    flux = face(cell(*left), cell(*fc, dc[0], dc[2]))
+                    out = []
+                    for f, g in ((0, 0), (1, 2), (2, 1)):
+                        q = pltpu.roll(edge[f], lanes - 1 - 2 * r, 1)
+                        low = jnp.where(lane_b == 0, q, flux[f])
+                        high = jnp.where(lane_b == lanes - 1, q, pltpu.roll(low, lanes - 1, 1))
+                        out.append((high - low + above[g] - below[g]) * (-1.0 / SPACING))
+                    finish(r, m, fc, out)
+                    fc, dc, below = fn, dn, above
             return carry
 
-        lax.fori_loop(0, blocks, body, 0)
+        lax.fori_loop(0, members // tall, body, 0)
 
     def finish1(r, m, fields, tend):
         for f in range(3):
@@ -244,6 +273,8 @@
             C[f, r, m, :] = 0.5 * (S[f, r, m, :] + fields[f] + STEP * tend[f])
 
     row_start(0, S)
+    for load in loads[1:]:
+        load.wait()
     META[OWN] = jnp.zeros((8, lanes), F32)
     META[OWN, 0:batches, 0:slots] = cells_ref[...].astype(F32)
     col_start(0, S)
@@ -288,10 +319,10 @@
         OBS[b, 1] = jnp.broadcast_to(column(wide(var_ref[b:b + 1, :])), (slots, lanes))
 
     col_wait(0)
-    advance(0, S, 1, rows - 1, finish1)
+    edge_flux(0)
+    advance(0, S, INNER, ((1, rows - 1),), finish1)
     row_wait(0, S)
-    advance(0, S, 0, 1, finish1)
-    advance(0, S, rows - 1, rows, finish1)
+    advance(0, S, OUTER, ((0, 1), (rows - 1, rows)), finish1)
 
     row_start(1, SEC)
     col_start(1, SEC)
@@ -330,10 +361,10 @@
                 TE[b, (k - 3) * slots:(k - 2) * slots, :] = t * t * (1.0 / members_1)
 
     col_wait(1)
-    advance(1, SEC, 1, rows - 1, finish2)
+    edge_flux(1)
+    advance(1, SEC, INNER, ((1, rows - 1),), finish2)
     row_wait(1, SEC)
-    advance(1, SEC, 0, 1, finish2)
-    advance(1, SEC, rows - 1, rows, finish2)
+    advance(1, SEC, OUTER, ((0, 1), (rows - 1, rows)), finish2)
 
     dot = functools.partial(lax.dot_general, preferred_element_type=F32)
     nn = (((1,), (0,)), ((), ()))
@@ -390,7 +421,8 @@
                 RC[f, pair] = centre(v)
             return carry
 
-        lax.fori_loop(0, 3, prepare, 0)
+        for f in range(3):
+            prepare(f, 0)
 
         def arrive(ks):
             for k, dr, dc in others:
@@ -411,7 +443,8 @@
                 C[f, 2 * pair + 1] = C[f, 2 * pair + 1] + inc[:, lanes:]
             return carry
 
-        lax.fori_loop(0, 3, update, 0)
+        for f in range(3):
+            update(f, 0)
         arrive((3, 4, 5, 6, 7, 8))
         anom_e, weight_e = operands(PK[b, 3:9].reshape(6 * slots, lanes))
 
@@ -427,21 +460,28 @@
                     out_ref[f, pl.ds(r, members, stride=rows), :] = done
             return carry
 
-        lax.fori_loop(0, 3, update_edges, 0)
+        for f in range(3):
+            update_edges(f, 0)
 
 
 def body(state, gauge_cells, gauge_count, obs_value, obs_noise, obs_var):
     fields, members, rows, lanes = state.shape
     batches, slots = gauge_cells.shape[2:]
     vmem = pl.BlockSpec(memory_space=pltpu.VMEM)
+    hbm = pl.BlockSpec(memory_space=pltpu.HBM)
     dma = pltpu.SemaphoreType.DMA
     grid = (fields, rows, members, lanes)
     out = pl.pallas_call(
         kernel,
         out_shape=jax.ShapeDtypeStruct((fields, members * rows, lanes), F32),
-        in_specs=[vmem, vmem, pl.BlockSpec(memory_space=pltpu.SMEM), vmem, vmem, vmem],
+        in_specs=[hbm, hbm, pl.BlockSpec(memory_space=pltpu.SMEM), hbm, hbm, hbm],
         out_specs=vmem,
         scratch_shapes=[
+            pltpu.VMEM((fields, members * rows, lanes), F32),
+            pltpu.VMEM((batches, slots), gauge_cells.dtype),
+            pltpu.VMEM((batches, slots), F32),
+            pltpu.VMEM((batches, slots, members), F32),
+            pltpu.VMEM((batches, slots), F32),
             pltpu.VMEM(grid, F32),
             pltpu.VMEM(grid, F32),
             pltpu.VMEM(grid, F32),
@@ -457,6 +497,7 @@
             pltpu.VMEM((fields, rows // 2, 4 * members, 2 * lanes), BF16),
             pltpu.VMEM((fields, 4 * members, lanes), BF16),
             pltpu.VMEM((fields, members, lanes), F32),
+            dma((5,)),
             dma((2, 2)), dma((2, 2)), dma((2, 2)), dma((2, 2)),
             dma((9,)), dma((9,)), dma((batches, 9)), dma((batches, 9)),
         ],

time: 47.4 us -> 33 us (0.70)
  Pallas kernels: 43.7 us -> 29.3 us
    pallas_call x1, Pallas kernels: 43.7 us -> 29.3 us  [body(): pl.pallas_call(kernel, out_shape=jax.ShapeDtypeStruct((fields, members *...]
where the time goes in v2:
time: 33 us; the launch traced here: 32.8 us
  Pallas kernels  29.3 us (89%)
  local copies, waits for them, and re-layouts  3.48 us (11%)
    pallas_call x1, Pallas kernels, body(): pl.pallas_call(kernel, out_shape=jax.ShapeDtypeStruct((fields, members *...  29.3 us
    unnamed x13, local copies, waits for them, and re-layouts  3.48 us

profile of v2, /device:TPU:0, one launch (start us, length us, event | category | flops | bytes accessed | tf_op | source)
XLA Modules:
  0.0 32.8 jit_solution(16333025891296790766)
XLA Ops:
  0.0 0.0 copy-start.3
  0.0 0.0 copy-start.4
  0.0 0.0 copy-start.2
  0.0 0.0 copy-start.5
  0.0 0.7 %copy-done.3 = f32[1,1,2,32]{3,2,1,0:T(2,128)S(1)} copy-done((f32[1,1,2,32]{3,2,1,0:T(2,128)S(1)}, f32[1,1,2,32]{3,2,1,0:T(2,128)}, u32[]{:S(2)}) %copy-start.3) | copy-done | bytes 280
  0.7 0.0 copy-done.4
  0.7 0.0 copy-done.2
  0.7 0.0 copy-done.5
  0.7 0.0 copy-start
  0.7 1.1 %copy-done = f32[3,64,8,128]{3,2,1,0:T(8,128)S(1)} copy-done((f32[3,64,8,128]{3,2,1,0:T(8,128)S(1)}, f32[3,64,8,128]{3,2,1,0:T(8,128)}, u32[]{:S(2)}) %copy-start) | copy-done | bytes 786456
  1.8 0.0 copy-start.1
  1.9 0.8 %copy-done.1 = f32[1,1,2,32,64]{4,3,2,1,0:T(8,128)S(1)} copy-done((f32[1,1,2,32,64]{4,3,2,1,0:T(8,128)S(1)}, f32[1,1,2,32,64]{4,3,2,1,0:T(8,128)}, u32[]{:S(2)}) %copy-start.1) | copy-done | bytes 16408
  2.6 29.3 %shard_map.64 = f32[3,512,128]{2,1,0:T(8,128)S(1)} custom-call(f32[3,512,128]{2,1,0:T(8,128)S(1)} %bitcast.7, s32[2,32]{1,0:T(2,128)S(1)} %bitcast.9, s32[1,1,2]{2,1,0:T(1,128)S(1)} %copy-done.5, f32[2,32]{1,0:T(2,128)S(1)} %bitcast.10, f32[2,32,64]{2,1,0:T(8,128)S(1)} %bitcast.8, f32[2,32]{1,0:T(2,128)S(1)} %bitcast.11), custom_call_target="tpu_custom_call" | custom-call | tf_op jit(solution)/shard_map/pallas_call | solution.py:474
  31.9 0.9 %copy.8 = f32[3,64,8,128]{3,2,1,0:T(8,128)} copy(f32[3,64,8,128]{3,2,1,0:T(8,128)S(1)} %bitcast.6) | data formatting | bytes 1572864
Async XLA Ops:
  0.0 0.7 %copy-start.3 = (f32[1,1,2,32]{3,2,1,0:T(2,128)S(1)}, f32[1,1,2,32]{3,2,1,0:T(2,128)}, u32[]{:S(2)}) copy-start(f32[1,1,2,32]{3,2,1,0:T(2,128)} %param.9) | copy-start | bytes 772
  0.0 0.7 %copy-start.4 = (f32[1,1,2,32]{3,2,1,0:T(2,128)S(1)}, f32[1,1,2,32]{3,2,1,0:T(2,128)}, u32[]{:S(2)}) copy-start(f32[1,1,2,32]{3,2,1,0:T(2,128)} %param.11) | copy-start | bytes 772
  0.0 0.7 %copy-start.2 = (s32[1,1,2,32]{3,2,1,0:T(2,128)S(1)}, s32[1,1,2,32]{3,2,1,0:T(2,128)}, u32[]{:S(2)}) copy-start(s32[1,1,2,32]{3,2,1,0:T(2,128)} %param.7) | copy-start | bytes 772
  0.0 0.7 %copy-start.5 = (s32[1,1,2]{2,1,0:T(1,128)S(1)}, s32[1,1,2]{2,1,0:T(1,128)}, u32[]{:S(2)}) copy-start(s32[1,1,2]{2,1,0:T(1,128)} %count_ref.1) | copy-start | bytes 28
  0.7 1.1 %copy-start = (f32[3,64,8,128]{3,2,1,0:T(8,128)S(1)}, f32[3,64,8,128]{3,2,1,0:T(8,128)}, u32[]{:S(2)}) copy-start(f32[3,64,8,128]{3,2,1,0:T(8,128)} %param.6) | copy-start | bytes 2359300
  1.8 0.8 %copy-start.1 = (f32[1,1,2,32,64]{4,3,2,1,0:T(8,128)S(1)}, f32[1,1,2,32,64]{4,3,2,1,0:T(8,128)}, u32[]{:S(2)}) copy-start(f32[1,1,2,32,64]{4,3,2,1,0:T(8,128)} %param.10) | copy-start | bytes 49156

commit v3 on v2

--- a/solution.py
+++ b/solution.py
@@ -13,7 +13,7 @@
 STEP = 0.08
 ROOT_G = GRAVITY ** 0.5
 INNER = 16
-OUTER = 32
+OUTER = 64
 F32 = jnp.float32
 BF16 = jnp.bfloat16
 MESH = pl.DeviceIdType.MESH
@@ -242,14 +242,15 @@
                 return cell(f[0], f[2], f[1], d[1], d[2])
 
             for first, last in spans:
-                fb = load(first - 1)
                 fc = load(first)
                 dc = derive(fc)
-                below = face(rowcell(fb, derive(fb)), rowcell(fc, dc))
+                below = None
                 for r in range(first, last):
-                    fn = load(r + 1)
-                    dn = derive(fn)
-                    above = face(rowcell(fc, dc), rowcell(fn, dn))
+                    fn = dn = above = None
+                    if r + 1 < last:
+                        fn = load(r + 1)
+                        dn = derive(fn)
+                        above = face(rowcell(fc, dc), rowcell(fn, dn))
                     left = [pltpu.roll(v, 1, 1) for v in (*fc, dc[0], dc[2])]
                     flux = face(cell(*left), cell(*fc, dc[0], dc[2]))
                     out = []
@@ -257,12 +258,35 @@
                         q = pltpu.roll(edge[f], lanes - 1 - 2 * r, 1)
                         low = jnp.where(lane_b == 0, q, flux[f])
                         high = jnp.where(lane_b == lanes - 1, q, pltpu.roll(low, lanes - 1, 1))
-                        out.append((high - low + above[g] - below[g]) * (-1.0 / SPACING))
+                        gain = high - low
+                        if above is not None:
+                            gain = gain + above[g]
+                        if below is not None:
+                            gain = gain - below[g]
+                        out.append(gain * (-1.0 / SPACING))
                     finish(r, m, fc, out)
                     fc, dc, below = fn, dn, above
             return carry
 
         lax.fori_loop(0, members // tall, body, 0)
+
+    def outer(stage, src, target, factor):
+        def body(i, carry):
+            m = pl.ds(pl.multiple_of(i * OUTER, 8), OUTER)
+
+            def rowcell(h, n, t):
+                rs = lax.rsqrt(h)
+                return cell(h, t, n, t * (rs * rs), ROOT_G * (h * rs))
+
+            for side, r, sign in ((0, 0, 1.0), (1, rows - 1, -1.0)):
+                ghost = rowcell(*(GR[stage, side, f, m, :] for f in range(3)))
+                inside = rowcell(*(src[f, r, m, :] for f in range(3)))
+                flux = face(ghost, inside) if side == 0 else face(inside, ghost)
+                for f, g in ((0, 0), (1, 2), (2, 1)):
+                    target[f, r, m, :] = target[f, r, m, :] + flux[g] * (sign * factor / SPACING)
+            return carry
+
+        lax.fori_loop(0, members // OUTER, body, 0)
 
     def finish1(r, m, fields, tend):
         for f in range(3):
@@ -320,9 +344,9 @@
 
     col_wait(0)
     edge_flux(0)
-    advance(0, S, INNER, ((1, rows - 1),), finish1)
+    advance(0, S, INNER, ((0, rows),), finish1)
     row_wait(0, S)
-    advance(0, S, OUTER, ((0, 1), (rows - 1, rows)), finish1)
+    outer(0, S, SEC, STEP)
 
     row_start(1, SEC)
     col_start(1, SEC)
@@ -362,9 +386,9 @@
 
     col_wait(1)
     edge_flux(1)
-    advance(1, SEC, INNER, ((1, rows - 1),), finish2)
+    advance(1, SEC, INNER, ((0, rows),), finish2)
     row_wait(1, SEC)
-    advance(1, SEC, OUTER, ((0, 1), (rows - 1, rows)), finish2)
+    outer(1, SEC, C, 0.5 * STEP)
 
     dot = functools.partial(lax.dot_general, preferred_element_type=F32)
     nn = (((1,), (0,)), ((), ()))
@@ -432,19 +456,21 @@
                         pk_copy(b, k, dr, dc).wait_send()
                         pk_copy(b, mirror(k), -dr, -dc).wait_recv()
 
-        arrive((0, 2))
-        anom_c, weight_c = operands(PK[b, 0:3].reshape(3 * slots, lanes))
-
-        def update(f, carry):
+        def update(f, anom_c, weight_c, taper):
             for pair in range(rows // 2):
                 span = slice(2 * pair * lanes, (2 * pair + 2) * lanes)
-                inc = increment(anom_c, weight_c, RC[f, pair], TC[b, :, span])
+                inc = increment(anom_c, weight_c, RC[f, pair], taper(span))
                 C[f, 2 * pair] = C[f, 2 * pair] + inc[:, :lanes]
                 C[f, 2 * pair + 1] = C[f, 2 * pair + 1] + inc[:, lanes:]
-            return carry
-
-        for f in range(3):
-            update(f, 0)
+
+        here = operands(PK[b, OWN])
+        for f in range(3):
+            update(f, *here, lambda span: TC[b, slots:2 * slots, span])
+        arrive((0, 2))
+        beside = operands(jnp.concatenate([PK[b, 0], PK[b, 2]], axis=0))
+        for f in range(3):
+            update(f, *beside, lambda span: jnp.concatenate(
+                [TC[b, :slots, span], TC[b, 2 * slots:, span]], axis=0))
         arrive((3, 4, 5, 6, 7, 8))
         anom_e, weight_e = operands(PK[b, 3:9].reshape(6 * slots, lanes))
 
@@ -502,7 +528,7 @@
             dma((9,)), dma((9,)), dma((batches, 9)), dma((batches, 9)),
         ],
         compiler_params=pltpu.CompilerParams(
-            collective_id=0, has_side_effects=True, vmem_limit_bytes=40 * 1024 * 1024),
+            collective_id=0, has_side_effects=True, vmem_limit_bytes=62 * 1024 * 1024),
     )(
         state.reshape(fields, members * rows, lanes),
         gauge_cells.reshape(batches, slots),

time: 33 us -> 31.6 us (0.958)
  local copies, waits for them, and re-layouts: 3.48 us -> 2.06 us
    unnamed x13 -> x1, local copies, waits for them, and re-layouts: 3.48 us -> 2.06 us
where the time goes in v3:
time: 31.6 us; the launch traced here: 31.4 us
  Pallas kernels  29.3 us (93%)
  local copies, waits for them, and re-layouts  2.06 us (7%)
    pallas_call x1, Pallas kernels, body(): pl.pallas_call(kernel, out_shape=jax.ShapeDtypeStruct((fields, members *...  29.3 us
    unnamed x1, local copies, waits for them, and re-layouts  2.06 us

profile of v3, /device:TPU:0, one launch (start us, length us, event | category | flops | bytes accessed | tf_op | source)
XLA Modules:
  0.0 31.4 jit_solution(9059768175302072025)
XLA Ops:
  0.0 29.3 %shard_map.64 = f32[3,512,128]{2,1,0:T(8,128)} custom-call(f32[3,512,128]{2,1,0:T(8,128)} %bitcast.7, s32[2,32]{1,0:T(2,128)} %bitcast.9, s32[1,1,2]{2,1,0:T(1,128)} %count_ref.1, f32[2,32]{1,0:T(2,128)} %bitcast.10, f32[2,32,64]{2,1,0:T(8,128)} %bitcast.8, f32[2,32]{1,0:T(2,128)} %bitcast.11), custom_call_target="tpu_custom_call" | custom-call | tf_op jit(solution)/shard_map/pallas_call | solution.py:500
  29.3 2.1 %copy.8 = f32[3,64,8,128]{3,2,1,0:T(8,128)} copy(f32[3,64,8,128]{3,2,1,0:T(8,128)} %bitcast.6) | data formatting | bytes 1572864
